TPU v7x, 32 devices: a whole 2x2x4 slice. The times are simulated.
32 devices in a mesh: node: 16 (over z, y, x), board: 2 (over core).
Axes of the slice: x: 2, y: 2, z: 4, core: 2. Of those that a mesh axis runs over, the one named last changes fastest.
Arguments:
- logits: float32 [2, 4, 512, 1326], P('board', None, 'node'), may hold values from -310 to 310
- pot_size: float32 [4, 512], P(None, 'node'), may hold values from 1 to 20
- node_type: int32 [4, 512], P(None, 'node'), may hold values from 0 to 2, as said below
- parent_slot: int32 [4, 512], P(None, 'node'), may hold values from 0 to 511, as said below
- range_one: float32 [2, 1326], P('board'), may hold values from 0.05 to 1
- range_two: float32 [2, 1326], P('board'), may hold values from 0.05 to 1
- hand_rank: int32 [2, 1326], P('board'), may hold values from 0 to 7461
- live_mask: int32 [2, 1326], P('board'), may hold values 0 or 1
Outputs:
- new_logits: float32 [2, 4, 512, 1326], P('board', None, 'node')
- values_half: float32 [2, 4, 512, 1326], P('board', None, 'node')
Inputs may be any that keep to these rules, and one draw needn't show every extreme that they name: `node_type`: 0 marks an inner node. At each level but the last, each aligned group of four slots holds exactly one node of type 0; the last level holds none. `parent_slot`: at level 0 every entry is 0. At a level above 0 the four nodes of an aligned group of four share one parent, a node of type 0 at the level before, and every such node is the parent of exactly one group; the parent's group index is the group's own index minus an offset of 0 to 7, one offset a level, modulo 512 / 4.
All inputs are finite; a program needn't handle non-finite values. No bound on the sum of `live_mask` on one device may be relied on, other than what follows from the above.
Results may differ from a plain program's by a relative error of at most 0.0003.
Values sent between devices are 32-bit elements; how exact they have to be, the bound alone decides.
No kernel may reach another device: no remote copies, remote signals or barrier semaphores. Data moves between devices by JAX's collectives and lax.ppermute only.
A program may use at most 64 MiB of HBM per device.

v0:
```python
import functools

import jax
import jax.numpy as jnp
import numpy as np
from jax import lax
from jax.experimental import pallas as pl
from jax.experimental.pallas import tpu as pltpu
from jax.sharding import PartitionSpec as P

LANES = 128
CARDS = 52
step_scale = 0.5
eps_value = 1e-06
MEBI = 1 << 20
CLASSES = (8, 10, 13, 16)
FAR = 5


def padded(count):
    return -(-count // LANES) * LANES


def card_rows(hand_count, wide):
    pairs = [(low, high) for low in range(CARDS) for high in range(low + 1, CARDS)]
    rows = np.full((2, wide), -1, np.int32)
    rows[:, :hand_count] = np.array(pairs[:hand_count], np.int32).T
    return rows


def payoff_kernel(hands, cards_ref, rank_ref, live_ref, out_ref, flat, left, right):
    wide = out_ref.shape[1]
    flat[...] = jnp.zeros(flat.shape, jnp.float32)
    flat[0:1, 0:hands] = rank_ref[...].astype(jnp.float32)
    flat[1:2, 0:hands] = (live_ref[...] > 0).astype(jnp.float32)
    dead = 1.0 - flat[1:2, :]
    feature = lax.broadcasted_iota(jnp.int32, (LANES, wide), 0)
    hit = (feature == cards_ref[0:1, :]) | (feature == cards_ref[1:2, :])
    base = jnp.where(hit, 1.0, 0.0)
    left[...] = jnp.where(feature == CARDS, dead, jnp.where(feature == CARDS + 1, 1.0, base))
    right[...] = jnp.where(
        feature == CARDS, 1.0, jnp.where(feature == CARDS + 1, dead, base)
    ).astype(jnp.bfloat16)
    rank_row = flat[0:1, :]
    for block in range(wide // LANES):
        part = slice(block * LANES, (block + 1) * LANES)
        left_block = left[:, part].T.astype(jnp.bfloat16)
        rank_col = jnp.broadcast_to(flat[0:1, part], (LANES, LANES)).T[:, 0:1]
        hits = jnp.dot(left_block, right[...], preferred_element_type=jnp.float32)
        compat = jnp.where(hits == 0.0, 1.0, 0.0)
        order = jnp.clip(rank_row - rank_col, -1.0, 1.0)
        out_ref[part, :] = (order * compat).astype(jnp.bfloat16)
        out_ref[wide + block * LANES : wide + (block + 1) * LANES, :] = compat.astype(jnp.bfloat16)


def payoff_blocks(hand_rank, live_mask):
    hands = hand_rank.shape[-1]
    wide = padded(hands)
    return pl.pallas_call(
        functools.partial(payoff_kernel, hands),
        out_shape=jax.ShapeDtypeStruct((2 * wide, wide), jnp.bfloat16),
        scratch_shapes=[
            pltpu.VMEM((8, wide), jnp.float32),
            pltpu.VMEM((LANES, wide), jnp.float32),
            pltpu.VMEM((LANES, wide), jnp.bfloat16),
        ],
        compiler_params=pltpu.CompilerParams(vmem_limit_bytes=20 * MEBI),
        cost_estimate=pl.CostEstimate(
            flops=2 * wide * wide * LANES, bytes_accessed=4 * wide * wide, transcendentals=0
        ),
        name="payoff",
    )(jnp.asarray(card_rows(hands, wide)), hand_rank, live_mask)


def row_count(planes, groups):
    return -(-planes * groups // 8) * 8


def plan_of(parent_ref, node_count, groups):
    total = groups * node_count
    first = lax.axis_index("node") * groups
    off = [lax.rem(first - (parent_ref[idx, 0] >> 2) + total, total) for idx in (1, 2, 3)]
    one = off[0]
    two = one + off[1]
    three = two + off[2]
    low = jnp.maximum(one, three - groups)
    high = jnp.minimum(two, groups)
    middle = jnp.minimum(jnp.maximum((one + two + three + 2) >> 2, low), high)
    return middle, middle - one, two - middle, three - middle


def class_of(shift, groups):
    need = jnp.maximum(shift[0] + shift[1], shift[2] + shift[3])
    found = jnp.int32(0)
    for size in CLASSES[:-1]:
        found = found + (need > size).astype(jnp.int32)
    return jnp.where(shift[3] > groups, len(CLASSES) - 1, found)


def fill_messages(node, stage, message_refs, size, block_ref, to_left, to_right):
    _, tiles, planes = stage.shape[:3]
    even = lax.rem(node, 2) == 0
    places = [(tile, plane) for tile in range(tiles) for plane in range(planes)]
    for side, on_left in enumerate((even, jnp.logical_not(even))):
        for near, far in zip(to_left, to_right):
            level = jnp.where(on_left, near[0], far[0])
            start = jnp.where(on_left, near[1], far[1])
            for tile, plane in places:
                stage[side, tile, plane, pl.ds(start, 8), :] = block_ref[level, tile, plane]
    for side, message_ref in enumerate(message_refs):
        for tile, plane in places:
            message_ref[tile, plane * size : plane * size + size, :] = stage[
                side, tile, plane, 8 : 8 + size, :
            ]


def prepare_kernel(
    node_count,
    parent_ref,
    logits_hbm,
    pot_ref,
    kind_ref,
    home_ref,
    shift_ref,
    class_ref,
    logits_ref,
    raw,
    flat,
    turned,
    sems,
):
    levels, tiles, planes, groups, _ = home_ref.shape
    slots = 4 * groups
    hands = logits_ref.shape[-1]
    fetches = [
        pltpu.make_async_copy(logits_hbm.at[0, idx], logits_ref.at[idx], sems.at[idx])
        for idx in range(levels)
    ]
    for fetch in fetches:
        fetch.start()
    shift = plan_of(parent_ref, node_count, groups)
    row_id = lax.broadcasted_iota(jnp.int32, shift_ref.shape, 0)
    spread = jnp.zeros(shift_ref.shape, jnp.int32)
    class_ref[...] = jnp.full((1, 1), class_of(shift, groups))
    for idx, value in enumerate(shift):
        spread = jnp.where(row_id == idx, value, spread)
    shift_ref[...] = spread
    pot = pot_ref[...]
    kind = kind_ref[...]
    level = lax.broadcasted_iota(jnp.int32, pot.shape, 0)
    sign = jnp.where(level % 2 == 0, -1.0, 1.0)
    flat[...] = jnp.zeros(flat.shape, jnp.float32)
    flat[0:levels, 0:slots] = jnp.where(kind == 2, pot, 0.0)
    flat[levels : 2 * levels, 0:slots] = jnp.where(kind == 1, pot, 0.0) * sign
    turned[...] = flat[...].T
    lane = lax.broadcasted_iota(jnp.int32, (groups, LANES), 1)
    for idx in range(levels):
        raw[idx, tiles - 1] = jnp.zeros((slots, LANES), jnp.float32)
    for idx in range(levels):
        fetches[idx].wait()
        for tile in range(tiles):
            start = tile * LANES
            stop = min(start + LANES, hands)
            raw[idx, tile, :, 0 : stop - start] = logits_ref[idx, :, start:stop]
            first = raw[idx, tile, pl.ds(0, groups, stride=4), :]
            for plane in range(planes):
                row = raw[idx, tile, pl.ds(plane + 1, groups, stride=4), :] - first
                if tile == tiles - 1 and plane == 0:
                    for slot in range(4):
                        scale = turned[pl.ds(slot, groups, stride=4), :]
                        row = jnp.where(lane == LANES - 8 + slot, scale[:, idx : idx + 1], row)
                        fold = scale[:, levels + idx : levels + idx + 1]
                        row = jnp.where(lane == LANES - 4 + slot, fold, row)
                home_ref[idx, tile, plane] = row


def prepared(logits, pot_size, node_type, parent_slot):
    _, levels, slots, hands = logits.shape
    groups = slots // 4
    tiles = padded(hands) // LANES
    vmem = pl.BlockSpec(memory_space=pltpu.VMEM)
    smem = pl.BlockSpec(memory_space=pltpu.SMEM)
    return pl.pallas_call(
        functools.partial(prepare_kernel, lax.axis_size("node")),
        out_shape=(
            jax.ShapeDtypeStruct((levels, tiles, 3, groups, LANES), jnp.float32),
            jax.ShapeDtypeStruct((8, LANES), jnp.int32),
            jax.ShapeDtypeStruct((1, 1), jnp.int32),
        ),
        in_specs=[smem, pl.BlockSpec(memory_space=pl.ANY), vmem, vmem],
        out_specs=(vmem, vmem, vmem),
        scratch_shapes=[
            pltpu.VMEM((levels, slots, hands), jnp.float32),
            pltpu.VMEM((levels, tiles, slots, LANES), jnp.float32),
            pltpu.VMEM((LANES, LANES), jnp.float32),
            pltpu.VMEM((LANES, LANES), jnp.float32),
            pltpu.SemaphoreType.DMA((levels,)),
        ],
        compiler_params=pltpu.CompilerParams(vmem_limit_bytes=10 * MEBI),
        name="prepare",
    )(parent_slot, logits, pot_size, node_type)


def ahead(rows, count):
    return pltpu.roll(rows, (8 - count) & 7, 0)


def behind(rows, count):
    return pltpu.roll(rows, count & 7, 0)


def shifts_in(shift_ref):
    return [jnp.max(shift_ref[idx : idx + 1, :]) for idx in range(4)]


def pack_kernel(size, far, shift_ref, home_ref, _pot, _kind, _parent, odd_ref, even_ref, *rest):
    far_ref = rest[0] if far else None
    stage = rest[-1]
    _, tiles, planes, groups, _ = home_ref.shape
    shift = shifts_in(shift_ref)
    fill_messages(
        lax.axis_index("node"),
        stage,
        (odd_ref, even_ref),
        size,
        home_ref,
        [(2, 8), (3, 8 + shift[2])],
        [(1, shift[0] + shift[1]), (0, shift[0])],
    )
    if far:
        for tile in range(tiles):
            for plane in range(planes):
                far_ref[tile, plane * FAR : plane * FAR + FAR, :] = home_ref[3, tile, plane, 0:FAR, :]


def message_shapes(planes, wide, size, far):
    tiles = wide // LANES
    message = jax.ShapeDtypeStruct((tiles, row_count(planes, size), LANES), jnp.float32)
    shapes = [message] * 2
    if far:
        shapes.append(jax.ShapeDtypeStruct((tiles, row_count(planes, FAR), LANES), jnp.float32))
    return shapes


def sent_on(odd, even, far, far_steps, order):
    count = lax.axis_size("node")
    edges = [(src, (src + 1) % count) for src in range(count)]
    got = [None, None]
    for side in order:
        pairs = [pair for edge in edges[1 - side :: 2] for pair in (edge, edge[::-1])]
        got[side] = lax.ppermute((odd, even)[side], "node", pairs)
    for message in far:
        pairs = [(src, (src + far_steps) % count) for src in range(count)]
        got.append(lax.ppermute(message, "node", pairs))
    return got


def spread_messages(node, from_left, from_right, odd_ref, even_ref, size):
    tiles, planes = from_left.shape[:2]
    even = lax.rem(node, 2) == 0
    for tile in range(tiles):
        for plane in range(planes):
            place = slice(plane * size, plane * size + size)
            odd_part = odd_ref[tile, place, :]
            even_part = even_ref[tile, place, :]
            from_left[tile, plane, 8 : 8 + size, :] = jnp.where(even, odd_part, even_part)
            from_right[tile, plane, 8 : 8 + size, :] = jnp.where(even, even_part, odd_part)


def inner_sum(inner, rows):
    total = jnp.where(inner[0], rows[0], 0.0)
    for idx in range(1, 4):
        total = total + jnp.where(inner[idx], rows[idx], 0.0)
    return total


def softmax_four(rows):
    top = jnp.maximum(jnp.maximum(rows[0], rows[1]), jnp.maximum(rows[2], 0.0))
    lifted = [jnp.exp(-top)] + [jnp.exp(row - top) for row in rows]
    total = (lifted[0] + lifted[1]) + (lifted[2] + lifted[3])
    return [row / total for row in lifted]


def operator_q(point, show, fold, range_one, range_two, block_ref, cols, put, top_ref=None):
    wide = block_ref.shape[1]
    inner = [
        [(show[idx][slot] == 0.0) & (fold[idx][slot] == 0.0) for slot in range(4)]
        for idx in range(4)
    ]
    strategy = [softmax_four(point[idx]) for idx in range(4)]
    top_one = [range_one * row for row in strategy[0]]
    above_one = inner_sum(inner[0], top_one)
    mid_two = [range_two * row for row in strategy[1]]
    above_two = inner_sum(inner[1], mid_two)
    low_one = [above_one * row for row in strategy[2]]
    last_one = inner_sum(inner[2], low_one)
    end_two = [above_two * row for row in strategy[3]]
    wide_two = jnp.broadcast_to(range_two, above_two.shape)
    units = [
        (0, [wide_two] * 4, 1.0, False),
        (1, mid_two, 1.0, True),
        (2, [above_two] * 4, 1.0, False),
        (3, end_two, 1.0, True),
        (1, [above_one] * 4, -1.0, False),
        (2, low_one, -1.0, True),
        (3, [last_one] * 4, -1.0, False),
    ]
    first_unit = 0 if top_ref is None else 1
    begin = [0] * len(units)
    place = 0
    for unit in range(first_unit, len(units)):
        idx, rows, fold_sign, as_sum = units[unit]
        begin[unit] = place
        for side in range(2):
            lanes = slice(side * wide, side * wide + wide)
            if side == 0:
                scaled = [rows[slot] * show[idx][slot] for slot in range(4)]
            else:
                scaled = [rows[slot] * (fold[idx][slot] * fold_sign) for slot in range(4)]
            if as_sum:
                rounded = [row.astype(jnp.bfloat16).astype(jnp.float32) for row in scaled]
                total = (rounded[0] + rounded[1]) + (rounded[2] + rounded[3])
                high = total.astype(jnp.bfloat16).astype(jnp.float32)
                scaled = [high, total - high]
            for pair in range(0, len(scaled), 2):
                cols[place + pair * 8 : place + pair * 8 + 16, lanes] = jnp.concatenate(
                    scaled[pair : pair + 2], axis=0
                ).astype(jnp.bfloat16)
        place += 16 if as_sum else 32

    def added(rows):
        return (rows[0] + rows[1]) + (rows[2] + rows[3])

    def landed(rows, kept, term):
        return [rows[slot] + jnp.where(kept[slot], term, 0.0) for slot in range(4)]

    total = None
    for start in range(0, wide, 2 * LANES):
        stop = min(start + 2 * LANES, wide)
        pay = jnp.dot(cols[...], block_ref[:, start:stop], preferred_element_type=jnp.float32)

        def paid(unit):
            at = begin[unit]
            return [pay[at + slot * 8 : at + slot * 8 + 8, :] for slot in range(4)]

        def paid_sum(unit):
            at = begin[unit]
            return pay[at : at + 8, :] + pay[at + 8 : at + 16, :]

        def weighed(idx, rows):
            return added([strategy[idx][slot][:, start:stop] * rows[slot] for slot in range(4)])

        value_two_end = paid(6)
        term_two = paid_sum(5) + weighed(3, value_two_end)
        value_two_mid = landed(paid(4), inner[1], term_two)
        value_one_low = landed(paid(2), inner[2], paid_sum(3))
        term_one = paid_sum(1) + weighed(2, value_one_low)
        if top_ref is None:
            value_one_top = landed(paid(0), inner[0], term_one)
        else:
            value_one_top = [
                jnp.where(inner[0][slot], term_one, top_ref[0, slot, :, start:stop])
                for slot in range(4)
            ]
        found = [value_one_top, value_two_mid, value_one_low, value_two_end]
        put(start, stop, found)
        part = squares(found)
        total = part if total is None else total + part
    return total


def squares(found):
    total = None
    for rows in found:
        for row in rows:
            total = row * row if total is None else total + row * row
    return jnp.broadcast_to(jnp.sum(total), (1, LANES))


def scale_columns(rows):
    wide = rows[0][0].shape[1]
    show = [
        [level[0][:, wide - 8 + slot : wide - 7 + slot] for slot in range(4)] for level in rows
    ]
    fold = [
        [level[0][:, wide - 4 + slot : wide - 4 + slot + 1] for slot in range(4)] for level in rows
    ]
    return show, fold


def wide_row(store, place, row_ref):
    hands = row_ref.shape[1]
    store[place : place + 1, 0:hands] = row_ref[...]
    return store[place : place + 1, :]


def first_kernel(size, far, shift_ref, home_ref, odd_ref, even_ref, *rest):
    if far:
        far_ref, rest = rest[0], rest[1:]
    one_ref, two_ref, block_ref, chain_ref, value_ref, square_ref = rest[:6]
    from_left, from_right, window, ranges, cols = rest[6:]
    _, tiles, planes, groups, _ = home_ref.shape
    shift = shifts_in(shift_ref)
    spread_messages(lax.axis_index("node"), from_left, from_right, odd_ref, even_ref, size)
    chain = lax.broadcasted_iota(jnp.int32, (groups, LANES), 0)
    places = [(tile, plane) for tile in range(tiles) for plane in range(planes)]
    if far:
        for tile, plane in places:
            window[tile, plane, 16 : 16 + FAR, :] = far_ref[
                tile, plane * FAR : plane * FAR + FAR, :
            ]
    point = [[[] for _ in range(planes)] for _ in range(4)]
    for tile, plane in places:
        top = jnp.where(
            chain < shift[0],
            from_left[tile, plane, 8:16, :],
            behind(home_ref[0, tile, plane], shift[0]),
        )
        mid = jnp.where(
            chain < shift[1],
            from_left[tile, plane, pl.ds(8 + shift[0], 8), :],
            behind(home_ref[1, tile, plane], shift[1]),
        )
        low = jnp.where(
            chain + shift[2] < 8,
            ahead(home_ref[2, tile, plane], shift[2]),
            from_right[tile, plane, pl.ds(shift[2], 8), :],
        )
        end = jnp.where(
            chain + shift[3] < 8,
            ahead(home_ref[3, tile, plane], shift[3]),
            from_right[tile, plane, pl.ds(shift[2] + shift[3], 8), :],
        )
        if far:
            far_part = window[tile, plane, pl.ds(shift[3], 8), :]
            end = jnp.where(chain + shift[3] < 16, end, far_part)
        for idx, row in enumerate((top, mid, low, end)):
            point[idx][plane].append(row)
    point = [[jnp.concatenate(rows, axis=1) for rows in level] for level in point]
    for idx in range(4):
        for plane in range(planes):
            chain_ref[idx, plane] = point[idx][plane]
    show, fold = scale_columns(point)
    ranges[...] = jnp.zeros(ranges.shape, jnp.float32)
    range_one = wide_row(ranges, 0, one_ref)
    range_two = wide_row(ranges, 1, two_ref)

    def put(start, stop, found):
        for idx in range(4):
            for slot in range(4):
                value_ref[idx, slot, :, start:stop] = found[idx][slot]

    square_ref[...] = operator_q(
        point, show, fold, range_one, range_two, block_ref, cols, put
    )


def rate_of(parts_ref, entry_count):
    square_sum = jnp.sum(parts_ref[...], axis=0, keepdims=True)[:, 0:1]
    return step_scale / jnp.sqrt(square_sum / entry_count + eps_value)


def second_kernel(entry_count, size, far, shift_ref, chain_ref, value_ref, *rest):
    parts_ref, one_ref, two_ref, block_ref, own_ref, odd_ref, even_ref = rest[:7]
    rest = rest[7:]
    if far:
        far_ref, rest = rest[0], rest[1:]
    square_ref, stage, ranges, cols = rest
    _, tiles, planes, groups, _ = own_ref.shape
    rate = rate_of(parts_ref, entry_count)
    raw = [[chain_ref[idx, plane] for plane in range(3)] for idx in range(4)]
    show, fold = scale_columns(raw)
    point = [
        [
            raw[idx][plane] + rate * (value_ref[idx, plane + 1] - value_ref[idx, 0])
            for plane in range(3)
        ]
        for idx in range(4)
    ]
    ranges[...] = jnp.zeros(ranges.shape, jnp.float32)
    range_one = wide_row(ranges, 0, one_ref)
    range_two = wide_row(ranges, 1, two_ref)

    def put(start, stop, found):
        for idx in range(4):
            for slot in range(4):
                for lane in range(start, stop, LANES):
                    row = found[idx][slot][:, lane - start : lane - start + LANES]
                    own_ref[idx, lane // LANES, slot] = row

    square_ref[...] = operator_q(
        point, show, fold, range_one, range_two, block_ref, cols, put, value_ref
    )
    shift = shifts_in(shift_ref)
    fill_messages(
        lax.axis_index("node"),
        stage,
        (odd_ref, even_ref),
        size,
        own_ref,
        [(0, 8), (1, 8 + shift[0])],
        [(3, shift[2] + shift[3]), (2, shift[2])],
    )
    if far:
        for tile in range(tiles):
            for plane in range(planes):
                part = stage.at[0, tile, plane]
                part[pl.ds(jnp.maximum(shift[3] - 8, 0), 8), :] = own_ref[3, tile, plane]
                far_ref[tile, plane * FAR : plane * FAR + FAR, :] = part[8 : 8 + FAR, :]


def last_kernel(entry_count, size, far, shift_ref, own_ref, even_ref, odd_ref, *rest):
    far_ref, rest = (rest[0], rest[1:]) if far else (None, rest)
    parts_ref, logits_hbm, new_hbm, half_hbm, from_left, from_right, lined = rest[:7]
    logits_ref, new_ref, half_ref, sems = rest[7:]
    levels, tiles, planes, groups, _ = own_ref.shape
    hands = logits_ref.shape[-1]
    fetches = [
        pltpu.make_async_copy(logits_hbm.at[0, idx], logits_ref.at[idx], sems.at[0, idx])
        for idx in range(levels)
    ]
    for fetch in fetches:
        fetch.start()
    shift = shifts_in(shift_ref)
    rate = rate_of(parts_ref, entry_count)
    group = lax.broadcasted_iota(jnp.int32, (groups, LANES), 0)
    spread_messages(lax.axis_index("node"), from_left, from_right, odd_ref, even_ref, size)
    places = [(tile, plane) for tile in range(tiles) for plane in range(planes)]

    def top(tile, plane, own):
        return jnp.where(
            group + shift[0] < 8,
            ahead(own, shift[0]),
            from_right[tile, plane, pl.ds(shift[0], 8), :],
        )

    def mid(tile, plane, own):
        return jnp.where(
            group + shift[1] < 8,
            ahead(own, shift[1]),
            from_right[tile, plane, pl.ds(shift[0] + shift[1], 8), :],
        )

    def low(tile, plane, own):
        return jnp.where(
            group < shift[2], from_left[tile, plane, 8:16, :], behind(own, shift[2])
        )

    def end(tile, plane, own):
        row = jnp.where(
            group < shift[3],
            from_left[tile, plane, pl.ds(8 + shift[2], 8), :],
            behind(own, shift[3]),
        )
        if far:
            far_part = far_ref[tile, plane * FAR : plane * FAR + 8, :]
            row = jnp.where(group < shift[3] - 8, far_part, row)
        return row

    leaving = []

    def leave(source, target, kind, idx):
        leaving.append(pltpu.make_async_copy(source.at[idx], target.at[0, idx], sems.at[kind, idx]))
        leaving[-1].start()

    for idx, found in enumerate((top, mid, low, end)):
        for tile, plane in places:
            row = found(tile, plane, own_ref[idx, tile, plane])
            lined[idx, tile, pl.ds(plane, groups, stride=4), :] = row
        fetches[idx].wait()
        for tile in range(tiles):
            start = tile * LANES
            stop = min(start + LANES, hands)
            value = lined[idx, tile][:, 0 : stop - start]
            half_ref[idx, :, start:stop] = value
            new_ref[idx, :, start:stop] = logits_ref[idx, :, start:stop] + rate * value
        leave(half_ref, half_hbm, 1, idx)
        leave(new_ref, new_hbm, 2, idx)
    for copy in leaving:
        copy.wait()


def shared_parts(part):
    count = lax.axis_size("node") * lax.axis_size("board")
    spread = jnp.broadcast_to(part, (count, LANES))
    return lax.all_to_all(spread, ("node", "board"), 0, 0, tiled=True)


def step_of_class(
    size,
    far,
    home,
    shift,
    logits,
    pot_size,
    node_type,
    parent_slot,
    range_one,
    range_two,
    hand_rank,
    live_mask,
):
    _, levels, slots, hands = logits.shape
    wide = padded(hands)
    tiles = wide // LANES
    groups = slots // 4
    entry_count = float(logits.size * lax.axis_size("node") * lax.axis_size("board"))
    vmem = pl.BlockSpec(memory_space=pltpu.VMEM)
    f32 = jnp.float32

    def limit(mebi):
        return pltpu.CompilerParams(vmem_limit_bytes=mebi * MEBI)

    def stage(planes, rows=32):
        return pltpu.VMEM((tiles, planes, rows, LANES), f32)

    def two_stages(planes):
        return pltpu.VMEM((2, tiles, planes, 32, LANES), f32)

    anywhere = pl.BlockSpec(memory_space=pl.ANY)
    sent = pl.pallas_call(
        functools.partial(pack_kernel, size, far),
        out_shape=message_shapes(3, wide, size, far),
        in_specs=[vmem, vmem] + [anywhere] * 3,
        scratch_shapes=[two_stages(3)],
        compiler_params=limit(8),
        name="pack",
    )(shift, home, pot_size, node_type, parent_slot)
    got = sent_on(sent[0], sent[1], sent[2:], -2, (0, 1))
    blocks = payoff_blocks(hand_rank, live_mask)
    rows = 4 * slots + 3 * 16

    def work(count):
        return [
            pltpu.VMEM((8, wide), f32),
            pltpu.VMEM((count, 2 * wide), jnp.bfloat16),
        ]

    def cost(count):
        return pl.CostEstimate(
            flops=4 * count * wide * wide, bytes_accessed=6 * wide * wide, transcendentals=0
        )

    square_shape = jax.ShapeDtypeStruct((1, LANES), f32)
    chain, value, part = pl.pallas_call(
        functools.partial(first_kernel, size, far),
        out_shape=(
            jax.ShapeDtypeStruct((levels, 3, groups, wide), f32),
            jax.ShapeDtypeStruct((levels, 4, groups, wide), f32),
            square_shape,
        ),
        in_specs=[vmem] * (5 + len(got)),
        scratch_shapes=[stage(3), stage(3), stage(3)] + work(rows),
        compiler_params=limit(32),
        cost_estimate=cost(rows),
        name="first",
    )(shift, home, *got, range_one, range_two, blocks)
    parts = shared_parts(part)
    own, *sent, part = pl.pallas_call(
        functools.partial(second_kernel, entry_count, size, far),
        out_shape=[jax.ShapeDtypeStruct((levels, tiles, 4, groups, LANES), f32)]
        + message_shapes(4, wide, size, far)
        + [square_shape],
        in_specs=[vmem] * 7,
        scratch_shapes=[two_stages(4)] + work(rows - slots),
        compiler_params=limit(32),
        cost_estimate=cost(rows - slots),
        name="second",
    )(shift, chain, value, parts, range_one, range_two, blocks)
    got = sent_on(sent[0], sent[1], sent[2:], 2, (1, 0))
    parts = shared_parts(part)
    out_shape = jax.ShapeDtypeStruct(logits.shape, f32)
    level_shape = (levels, slots, hands)
    return pl.pallas_call(
        functools.partial(last_kernel, entry_count, size, far),
        out_shape=(out_shape, out_shape),
        in_specs=[vmem] * (3 + len(got)) + [anywhere],
        out_specs=(anywhere, anywhere),
        scratch_shapes=[
            stage(4),
            stage(4),
            pltpu.VMEM((levels, tiles, slots, LANES), f32),
            pltpu.VMEM(level_shape, f32),
            pltpu.VMEM(level_shape, f32),
            pltpu.VMEM(level_shape, f32),
            pltpu.SemaphoreType.DMA((3, levels)),
        ],
        compiler_params=limit(24),
        name="last",
    )(shift, own, got[1], got[0], *got[2:], parts, logits)


def per_device(
    logits, pot_size, node_type, parent_slot, range_one, range_two, hand_rank, live_mask
):
    branches = [
        functools.partial(step_of_class, size, size == CLASSES[-1]) for size in CLASSES
    ]
    home, shift, found = prepared(logits, pot_size, node_type, parent_slot)
    return lax.switch(
        found[0, 0],
        branches,
        home,
        shift,
        logits,
        pot_size,
        node_type,
        parent_slot,
        range_one,
        range_two,
        hand_rank,
        live_mask,
    )


def solution(mesh):
    return jax.shard_map(
        per_device,
        mesh=mesh,
        in_specs=(
            P("board", None, "node", None),
            P(None, "node"),
            P(None, "node"),
            P(None, "node"),
            P("board", None),
            P("board", None),
            P("board", None),
            P("board", None),
        ),
        out_specs=(P("board", None, "node", None), P("board", None, "node", None)),
        check_vma=False,
    )
```

profile of v0, /device:TPU:0, one launch (start us, length us, event | category | flops | bytes accessed | tf_op | source)
XLA Modules:
  0.0 50.6 jit_solution(1327319249953739046)
XLA Ops:
  0.6 2.5 %prepare.1 = (f32[4,11,3,8,128]{4,3,2,1,0:T(8,128)S(1)}, s32[8,128]{1,0:T(8,128)S(1)}, s32[1,1]{1,0:T(1,128)}) custom-call(s32[4,32]{1,0:T(4,128)} %parent_ref.1, f32[1,4,32,1326]{3,2,1,0:T(8,128)} %logits_hbm.1, f32[4,32]{1,0:T(4,128)} %pot_ref.1, s32[4,32]{1,0:T(4,128)} %kind_ref.1), custom_call_target="tpu_custom_call" | custom-call | tf_op jit(solution)/shard_map/prepare/pallas_call | solution.py:183
  3.8 46.6 %conditional.1 = ((f32[1,4,32,1326]{3,2,1,0:T(8,128)}, f32[1,4,32,1326]{3,2,1,0:T(8,128)})) conditional(s32[]{:T(128)} %bitcast.16, (s32[8,128]{1,0:T(8,128)S(1)}, f32[4,11,3,8,128]{4,3,2,1,0:T(8,128)S(1)}, f32[4,32]{1,0:T(4,128)}, s32[4,32]{1,0:T(4,128)}, s32[4,32]{1,0:T(4,128)}, /*index=5*/s32[2,1408]{1,0:T(2,128)}, ...), branch_computations={%region_0.0_spmd, %region_1.0_spmd, %region_2.0_spmd, %region_3.0_... | conditional | flops 3045064704 | bytes 40524556 | solution.py:700
  4.0 0.0 copy-start.5
  4.0 0.0 copy-start.9
  4.0 0.3 pack.5
  4.3 7.0 %collective-permute-start.4 = (f32[11,32,128]{2,1,0:T(8,128)S(1)}, f32[11,32,128]{2,1,0:T(8,128)S(1)}, u32[]{:S(2)}, u32[]{:S(2)}) collective-permute-start(f32[11,32,128]{2,1,0:T(8,128)S(1)} %get-tuple-element.113), channel_id=1, source_target_pairs={{2,4},{4,2},{6,8},{8,6},{10,12},{12,10},{14,16},{16,14},{18,20},{2... | collective-permute-start | bytes 540680 | tf_op jit(solution)/shard_map/cond/branch_1_fun/ppermute | solution.py:251
  11.3 0.0 collective-permute-start.5
  11.3 2.8 %payoff.5.rest_2_.rest_3_ = bf16[2816,1408]{1,0:T(8,128)(2,1)S(1)} custom-call(s32[2,1408]{1,0:T(2,128)} %get-tuple-element.117.cards_ref, s32[1,1326]{1,0:T(1,128)} %get-tuple-element.118.rank_ref, s32[1,1326]{1,0:T(1,128)} %get-tuple-element.119.live_ref), custom_call_target="tpu_custom_call" | custom-call | flops 507510784 | bytes 7929856 | tf_op jit(solution)/shard_map/cond/branch_1_fun/payoff/pallas_call | solution.py:59
  14.2 1.8 %collective-permute-done.4.odd_ref = f32[11,32,128]{2,1,0:T(8,128)S(1)} collective-permute-done((f32[11,32,128]{2,1,0:T(8,128)S(1)}, f32[11,32,128]{2,1,0:T(8,128)S(1)}, u32[]{:S(2)}, u32[]{:S(2)}) %collective-permute-start.4) | collective-permute-done | bytes 180256 | tf_op jit(solution)/shard_map/cond/branch_1_fun/ppermute | solution.py:251
  16.0 1.4 %collective-permute-done.5.even_ref = f32[11,32,128]{2,1,0:T(8,128)S(1)} collective-permute-done((f32[11,32,128]{2,1,0:T(8,128)S(1)}, f32[11,32,128]{2,1,0:T(8,128)S(1)}, u32[]{:S(2)}, u32[]{:S(2)}) %collective-permute-start.5) | collective-permute-done | bytes 180256 | tf_op jit(solution)/shard_map/cond/branch_1_fun/ppermute | solution.py:251
  17.3 0.0 copy-done.5
  17.3 0.0 copy-done.9
  17.3 0.0 copy-start.1
  17.3 2.5 %first.5 = (f32[4,3,8,1408]{3,2,1,0:T(8,128)S(1)}, f32[4,4,8,1408]{3,2,1,0:T(8,128)S(1)}, f32[1,128]{1,0:T(1,128)S(1)}) custom-call(s32[8,128]{1,0:T(8,128)S(1)} %get-tuple-element.108.shift_ref, f32[4,11,3,8,128]{4,3,2,1,0:T(8,128)S(1)} %get-tuple-element.109.home_ref, f32[11,32,128]{2,1,0:T(8,128)S(1)} %collective-permute-done.4.odd_ref, ...), custom_call_target="tpu_custom_call" | custom-call | flops 1395654656 | bytes 11894784 | tf_op jit(solution)/shard_map/cond/branch_1_fun/first/pallas_call | solution.py:645
  19.9 11.7 %all_to_all.50 = f32[32,1,128]{2,1,0:T(1,128)S(1)} all-to-all(f32[32,1,128]{2,1,0:T(1,128)S(1)} %broadcast_in_dim.16), channel_id=1, replica_groups=mesh['node'=16,'board'=2] {'node','board'}, dimensions={0} | all-to-all | bytes 32768 | tf_op jit(solution)/shard_map/cond/branch_1_fun/all_to_all | solution.py:586
  31.6 2.3 %second.5 = (f32[4,11,4,8,128]{4,3,2,1,0:T(8,128)S(1)}, f32[11,40,128]{2,1,0:T(8,128)S(1)}, f32[11,40,128]{2,1,0:T(8,128)S(1)}, f32[1,128]{1,0:T(1,128)S(1)}) custom-call(s32[8,128]{1,0:T(8,128)S(1)} %get-tuple-element.108.shift_ref, f32[4,3,8,1408]{3,2,1,0:T(8,128)S(1)} %get-tuple-element.120.chain_ref, f32[4,4,8,1408]{3,2,1,0:T(8,128)S(1)} %get-tuple-element.121.value_ref, ...), custom_call_target="tpu_custom_call" | custom-call | flops 1141899264 | bytes 11894784 | tf_op jit(solution)/shard_map/cond/branch_1_fun/second/pallas_call | solution.py:659
  33.9 0.6 %collective-permute-start.6 = (f32[11,40,128]{2,1,0:T(8,128)S(1)}, f32[11,40,128]{2,1,0:T(8,128)S(1)}, u32[]{:S(2)}, u32[]{:S(2)}) collective-permute-start(f32[11,40,128]{2,1,0:T(8,128)S(1)} %get-tuple-element.124), channel_id=1, source_target_pairs={{0,2},{2,0},{4,6},{6,4},{8,10},{10,8},{12,14},{14,12},{16,18},{18,... | collective-permute-start | bytes 675848 | tf_op jit(solution)/shard_map/cond/branch_1_fun/ppermute | solution.py:251
  34.5 1.5 %collective-permute-start.7 = (f32[11,40,128]{2,1,0:T(8,128)S(1)}, f32[11,40,128]{2,1,0:T(8,128)S(1)}, u32[]{:S(2)}, u32[]{:S(2)}) collective-permute-start(f32[11,40,128]{2,1,0:T(8,128)S(1)} %get-tuple-element.125), channel_id=1, source_target_pairs={{2,4},{4,2},{6,8},{8,6},{10,12},{12,10},{14,16},{16,14},{18,20},{2... | collective-permute-start | bytes 675848 | tf_op jit(solution)/shard_map/cond/branch_1_fun/ppermute | solution.py:251
  36.0 11.5 %all_to_all.51 = f32[32,1,128]{2,1,0:T(1,128)S(1)} all-to-all(f32[32,1,128]{2,1,0:T(1,128)S(1)} %broadcast_in_dim.17), channel_id=1, replica_groups=mesh['node'=16,'board'=2] {'node','board'}, dimensions={0} | all-to-all | bytes 32768 | tf_op jit(solution)/shard_map/cond/branch_1_fun/all_to_all | solution.py:586
  47.5 0.0 collective-permute-done.6.even_ref
  47.5 0.0 collective-permute-done.7.odd_ref
  47.5 0.0 copy-done.1
  47.5 2.4 %last.5 = (f32[1,4,32,1326]{3,2,1,0:T(8,128)}, f32[1,4,32,1326]{3,2,1,0:T(8,128)}) custom-call(s32[8,128]{1,0:T(8,128)S(1)} %get-tuple-element.108.shift_ref, f32[4,11,4,8,128]{4,3,2,1,0:T(8,128)S(1)} %get-tuple-element.123.own_ref, f32[11,40,128]{2,1,0:T(8,128)S(1)} %collective-permute-done.6.even_ref, f32[11,40,128]{2,1,0:T(8,128)S(1)} %collective-permute-done.7.odd_ref, ...), custom_call_target="tpu_custom_call" | custom-call | tf_op jit(solution)/shard_map/cond/branch_1_fun/last/pallas_call | solution.py:674
  (2 shorter events, 0.0 us)
Async XLA Ops:
  4.0 13.4 %copy-start.5 = (f32[1,1326]{1,0:T(1,128)S(1)}, f32[1,1326]{1,0:T(1,128)}, u32[]{:S(2)}) copy-start(f32[1,1326]{1,0:T(1,128)} %get-tuple-element.115.rest_0_.rest_1_) | copy-start | bytes 15916 | tf_op jit(solution)/shard_map/cond
  4.0 13.3 %copy-start.9 = (f32[1,1326]{1,0:T(1,128)S(1)}, f32[1,1326]{1,0:T(1,128)}, u32[]{:S(2)}) copy-start(f32[1,1326]{1,0:T(1,128)} %get-tuple-element.116.rest_1_.rest_2_) | copy-start | bytes 15916 | tf_op jit(solution)/shard_map/cond
  4.3 11.7 %collective-permute-start.4 = (f32[11,32,128]{2,1,0:T(8,128)S(1)}, f32[11,32,128]{2,1,0:T(8,128)S(1)}, u32[]{:S(2)}, u32[]{:S(2)}) collective-permute-start(f32[11,32,128]{2,1,0:T(8,128)S(1)} %get-tuple-element.113), channel_id=1, source_target_pairs={{2,4},{4,2},{6,8},{8,6},{10,12},{12,10},{14,16},{16,14},{18,20},{2... | collective-permute-start | bytes 540680 | tf_op jit(solution)/shard_map/cond/branch_1_fun/ppermute | solution.py:251
  11.3 6.0 %collective-permute-start.5 = (f32[11,32,128]{2,1,0:T(8,128)S(1)}, f32[11,32,128]{2,1,0:T(8,128)S(1)}, u32[]{:S(2)}, u32[]{:S(2)}) collective-permute-start(f32[11,32,128]{2,1,0:T(8,128)S(1)} %get-tuple-element.114), channel_id=1, source_target_pairs={{0,2},{2,0},{4,6},{6,4},{8,10},{10,8},{12,14},{14,12},{16,18},{18,... | collective-permute-start | bytes 540680 | tf_op jit(solution)/shard_map/cond/branch_1_fun/ppermute | solution.py:251
  17.3 30.1 %copy-start.1 = (f32[1,4,32,1326]{3,2,1,0:T(8,128)S(1)}, f32[1,4,32,1326]{3,2,1,0:T(8,128)}, u32[]{:S(2)}) copy-start(f32[1,4,32,1326]{3,2,1,0:T(8,128)} %get-tuple-element.127.rest_1_) | copy-start | bytes 2036740 | tf_op jit(solution)/shard_map/cond
  33.9 13.6 %collective-permute-start.6 = (f32[11,40,128]{2,1,0:T(8,128)S(1)}, f32[11,40,128]{2,1,0:T(8,128)S(1)}, u32[]{:S(2)}, u32[]{:S(2)}) collective-permute-start(f32[11,40,128]{2,1,0:T(8,128)S(1)} %get-tuple-element.124), channel_id=1, source_target_pairs={{0,2},{2,0},{4,6},{6,4},{8,10},{10,8},{12,14},{14,12},{16,18},{18,... | collective-permute-start | bytes 675848 | tf_op jit(solution)/shard_map/cond/branch_1_fun/ppermute | solution.py:251
  34.5 13.0 %collective-permute-start.7 = (f32[11,40,128]{2,1,0:T(8,128)S(1)}, f32[11,40,128]{2,1,0:T(8,128)S(1)}, u32[]{:S(2)}, u32[]{:S(2)}) collective-permute-start(f32[11,40,128]{2,1,0:T(8,128)S(1)} %get-tuple-element.125), channel_id=1, source_target_pairs={{2,4},{4,2},{6,8},{8,6},{10,12},{12,10},{14,16},{16,14},{18,20},{2... | collective-permute-start | bytes 675848 | tf_op jit(solution)/shard_map/cond/branch_1_fun/ppermute | solution.py:251
where the time goes:
time: 50.9 us; the launch traced here: 50.6 us
  blocking collectives  23.2 us (46%)
  Pallas kernels  12.8 us (25%)
  starting transfers between devices  9.06 us (18%)
  waiting for transfers between devices  3.16 us (6%)
  between operations  1.51 us (3%)
  loops' own time  0.8 us (2%)
    all_to_all x2, blocking collectives, shared_parts(): return lax.all_to_all(spread, ('node', 'board'), 0, 0, tiled=True)  23.2 us
    ppermute x4, starting transfers between devices, sent_on(): got[side] = lax.ppermute((odd, even)[side], 'node', pairs)  9.06 us
    ppermute x4, waiting for transfers between devices, sent_on(): got[side] = lax.ppermute((odd, even)[side], 'node', pairs)  3.16 us
    pallas_call x1, Pallas kernels, payoff_blocks(): pl.pallas_call(functools.partial(payoff_kernel, hands), out_shape=jax.Sha...  2.85 us
    pallas_call x1, Pallas kernels, step_of_class(): pl.pallas_call(functools.partial(first_kernel, size, far), out_shape=(jax...  2.54 us
    pallas_call x1, Pallas kernels, prepared(): pl.pallas_call(functools.partial(prepare_kernel, lax.axis_size('node')),...  2.5 us
    pallas_call x1, Pallas kernels, step_of_class(): pl.pallas_call(functools.partial(last_kernel, entry_count, size, far), ou...  2.37 us
    pallas_call x1, Pallas kernels, step_of_class(): pl.pallas_call(functools.partial(second_kernel, entry_count, size, far),...  2.27 us
  transfers between devices with their start and end apart: 4, of which 2 were waited for; matrix products, arithmetic and copies ran while one was open for 0% of the time, Pallas kernels for 6%

commit v1 on v0

--- a/solution.py
+++ b/solution.py
@@ -13,7 +13,7 @@
 step_scale = 0.5
 eps_value = 1e-06
 MEBI = 1 << 20
-CLASSES = (8, 10, 13, 16)
+CLASSES = (8, 10, 12, 14)
 FAR = 5
 
 
@@ -90,14 +90,17 @@
 
 
 def class_of(shift, groups):
-    need = jnp.maximum(shift[0] + shift[1], shift[2] + shift[3])
+    near = jnp.where(shift[3] > groups, 2 * groups - shift[3], shift[3])
+    need = jnp.maximum(shift[0] + shift[1], shift[2] + near)
     found = jnp.int32(0)
     for size in CLASSES[:-1]:
         found = found + (need > size).astype(jnp.int32)
     return jnp.where(shift[3] > groups, len(CLASSES) - 1, found)
 
 
-def fill_messages(node, stage, message_refs, size, block_ref, to_left, to_right):
+def fill_messages(
+    node, stage, message_refs, size, block_ref, to_left, to_right, skipped=None
+):
     _, tiles, planes = stage.shape[:3]
     even = lax.rem(node, 2) == 0
     places = [(tile, plane) for tile in range(tiles) for plane in range(planes)]
@@ -106,7 +109,10 @@
             level = jnp.where(on_left, near[0], far[0])
             start = jnp.where(on_left, near[1], far[1])
             for tile, plane in places:
-                stage[side, tile, plane, pl.ds(start, 8), :] = block_ref[level, tile, plane]
+                block = block_ref[level, tile, plane]
+                if skipped is not None:
+                    block = ahead(block, jnp.where(level == 3, skipped, 0))
+                stage[side, tile, plane, pl.ds(start, 8), :] = block
     for side, message_ref in enumerate(message_refs):
         for tile, plane in places:
             message_ref[tile, plane * size : plane * size + size, :] = stage[
@@ -116,14 +122,17 @@
 
 def prepare_kernel(
     node_count,
-    parent_ref,
+    parent_hbm,
     logits_hbm,
-    pot_ref,
-    kind_ref,
+    pot_hbm,
+    kind_hbm,
     home_ref,
     shift_ref,
     class_ref,
+    parent_ref,
     logits_ref,
+    pot_ref,
+    kind_ref,
     raw,
     flat,
     turned,
@@ -136,8 +145,16 @@
         pltpu.make_async_copy(logits_hbm.at[0, idx], logits_ref.at[idx], sems.at[idx])
         for idx in range(levels)
     ]
-    for fetch in fetches:
+    tables = [
+        pltpu.make_async_copy(source, target, sems.at[levels + idx])
+        for idx, (source, target) in enumerate(
+            ((parent_hbm, parent_ref), (pot_hbm, pot_ref), (kind_hbm, kind_ref))
+        )
+    ]
+    for fetch in tables + fetches:
         fetch.start()
+    for fetch in tables:
+        fetch.wait()
     shift = plan_of(parent_ref, node_count, groups)
     row_id = lax.broadcasted_iota(jnp.int32, shift_ref.shape, 0)
     spread = jnp.zeros(shift_ref.shape, jnp.int32)
@@ -179,7 +196,6 @@
     groups = slots // 4
     tiles = padded(hands) // LANES
     vmem = pl.BlockSpec(memory_space=pltpu.VMEM)
-    smem = pl.BlockSpec(memory_space=pltpu.SMEM)
     return pl.pallas_call(
         functools.partial(prepare_kernel, lax.axis_size("node")),
         out_shape=(
@@ -187,14 +203,17 @@
             jax.ShapeDtypeStruct((8, LANES), jnp.int32),
             jax.ShapeDtypeStruct((1, 1), jnp.int32),
         ),
-        in_specs=[smem, pl.BlockSpec(memory_space=pl.ANY), vmem, vmem],
+        in_specs=[pl.BlockSpec(memory_space=pl.ANY)] * 4,
         out_specs=(vmem, vmem, vmem),
         scratch_shapes=[
+            pltpu.SMEM(parent_slot.shape, jnp.int32),
             pltpu.VMEM((levels, slots, hands), jnp.float32),
+            pltpu.VMEM(pot_size.shape, jnp.float32),
+            pltpu.VMEM(node_type.shape, jnp.int32),
             pltpu.VMEM((levels, tiles, slots, LANES), jnp.float32),
             pltpu.VMEM((LANES, LANES), jnp.float32),
             pltpu.VMEM((LANES, LANES), jnp.float32),
-            pltpu.SemaphoreType.DMA((levels,)),
+            pltpu.SemaphoreType.DMA((levels + 3,)),
         ],
         compiler_params=pltpu.CompilerParams(vmem_limit_bytes=10 * MEBI),
         name="prepare",
@@ -218,6 +237,7 @@
     stage = rest[-1]
     _, tiles, planes, groups, _ = home_ref.shape
     shift = shifts_in(shift_ref)
+    skipped = jnp.maximum(shift[3] - 8, 0) if far else None
     fill_messages(
         lax.axis_index("node"),
         stage,
@@ -226,6 +246,7 @@
         home_ref,
         [(2, 8), (3, 8 + shift[2])],
         [(1, shift[0] + shift[1]), (0, shift[0])],
+        skipped,
     )
     if far:
         for tile in range(tiles):
@@ -429,7 +450,7 @@
         end = jnp.where(
             chain + shift[3] < 8,
             ahead(home_ref[3, tile, plane], shift[3]),
-            from_right[tile, plane, pl.ds(shift[2] + shift[3], 8), :],
+            from_right[tile, plane, pl.ds(shift[2] + jnp.minimum(shift[3], 8), 8), :],
         )
         if far:
             far_part = window[tile, plane, pl.ds(shift[3], 8), :]
@@ -499,7 +520,7 @@
         size,
         own_ref,
         [(0, 8), (1, 8 + shift[0])],
-        [(3, shift[2] + shift[3]), (2, shift[2])],
+        [(3, shift[2] + jnp.minimum(shift[3], 8)), (2, shift[2])],
     )
     if far:
         for tile in range(tiles):
@@ -549,7 +570,7 @@
     def end(tile, plane, own):
         row = jnp.where(
             group < shift[3],
-            from_left[tile, plane, pl.ds(8 + shift[2], 8), :],
+            from_left[tile, plane, pl.ds(8 + shift[2] - jnp.maximum(shift[3] - 8, 0), 8), :],
             behind(own, shift[3]),
         )
         if far:

time: 50.9 us -> 48.6 us (0.955)
  waiting for transfers between devices: 3.16 us -> 2.19 us
  Pallas kernels: 12.8 us -> 12.2 us
    ppermute x4, waiting for transfers between devices: 3.16 us -> 2.19 us  [sent_on(): got[side] = lax.ppermute((odd, even)[side], 'node', pairs)]
    pallas_call x1, Pallas kernels: 2.5 us -> 1.82 us  [prepared(): pl.pallas_call(functools.partial(prepare_kernel, lax.axis_size('node')),...]
where the time goes in v1:
time: 48.6 us; the launch traced here: 48.4 us
  blocking collectives  22.8 us (47%)
  Pallas kernels  12.2 us (25%)
  starting transfers between devices  9.06 us (19%)
  waiting for transfers between devices  2.19 us (5%)
  between operations  1.51 us (3%)
  loops' own time  0.62 us (1%)
    all_to_all x2, blocking collectives, shared_parts(): return lax.all_to_all(spread, ('node', 'board'), 0, 0, tiled=True)  22.8 us
    ppermute x4, starting transfers between devices, sent_on(): got[side] = lax.ppermute((odd, even)[side], 'node', pairs)  9.06 us
    pallas_call x1, Pallas kernels, payoff_blocks(): pl.pallas_call(functools.partial(payoff_kernel, hands), out_shape=jax.Sha...  2.84 us
    pallas_call x1, Pallas kernels, step_of_class(): pl.pallas_call(functools.partial(first_kernel, size, far), out_shape=(jax...  2.55 us
    pallas_call x1, Pallas kernels, step_of_class(): pl.pallas_call(functools.partial(last_kernel, entry_count, size, far), ou...  2.37 us
    pallas_call x1, Pallas kernels, step_of_class(): pl.pallas_call(functools.partial(second_kernel, entry_count, size, far),...  2.28 us
    ppermute x4, waiting for transfers between devices, sent_on(): got[side] = lax.ppermute((odd, even)[side], 'node', pairs)  2.19 us
    pallas_call x1, Pallas kernels, prepared(): pl.pallas_call(functools.partial(prepare_kernel, lax.axis_size('node')),...  1.82 us
  transfers between devices with their start and end apart: 4, of which 2 were waited for; matrix products, arithmetic and copies ran while one was open for 0% of the time, Pallas kernels for 6%

profile of v1, /device:TPU:0, one launch (start us, length us, event | category | flops | bytes accessed | tf_op | source)
XLA Modules:
  0.0 48.4 jit_solution(14954972468715189897)
XLA Ops:
  0.6 1.8 %prepare.1 = (f32[4,11,3,8,128]{4,3,2,1,0:T(8,128)S(1)}, s32[8,128]{1,0:T(8,128)S(1)}, s32[1,1]{1,0:T(1,128)}) custom-call(s32[4,32]{1,0:T(4,128)} %parent_hbm.1, f32[1,4,32,1326]{3,2,1,0:T(8,128)} %logits_hbm.1, f32[4,32]{1,0:T(4,128)} %pot_hbm.1, s32[4,32]{1,0:T(4,128)} %kind_hbm.1), custom_call_target="tpu_custom_call" | custom-call | tf_op jit(solution)/shard_map/prepare/pallas_call | solution.py:199
  3.1 45.1 %conditional.1 = ((f32[1,4,32,1326]{3,2,1,0:T(8,128)}, f32[1,4,32,1326]{3,2,1,0:T(8,128)})) conditional(s32[]{:T(128)} %bitcast.16, (s32[8,128]{1,0:T(8,128)S(1)}, f32[4,11,3,8,128]{4,3,2,1,0:T(8,128)S(1)}, f32[4,32]{1,0:T(4,128)}, s32[4,32]{1,0:T(4,128)}, s32[4,32]{1,0:T(4,128)}, /*index=5*/s32[2,1408]{1,0:T(2,128)}, ...), branch_computations={%region_0.0_spmd, %region_1.0_spmd, %region_2.0_spmd, %region_3.0_... | conditional | flops 3045064704 | bytes 40164108 | solution.py:721
  3.1 0.0 copy-start.4
  3.1 0.0 copy-start.8
  3.1 0.3 pack.4
  3.5 7.0 %collective-permute-start = (f32[11,24,128]{2,1,0:T(8,128)S(1)}, f32[11,24,128]{2,1,0:T(8,128)S(1)}, u32[]{:S(2)}, u32[]{:S(2)}) collective-permute-start(f32[11,24,128]{2,1,0:T(8,128)S(1)} %get-tuple-element.93), channel_id=1, source_target_pairs={{2,4},{4,2},{6,8},{8,6},{10,12},{12,10},{14,16},{16,14},{18,20},{2... | collective-permute-start | bytes 405512 | tf_op jit(solution)/shard_map/cond/branch_0_fun/ppermute | solution.py:272
  10.5 0.0 collective-permute-start.1
  10.5 2.8 %payoff.4.rest_2_.rest_3_ = bf16[2816,1408]{1,0:T(8,128)(2,1)S(1)} custom-call(s32[2,1408]{1,0:T(2,128)} %get-tuple-element.97.cards_ref, s32[1,1326]{1,0:T(1,128)} %get-tuple-element.98.rank_ref, s32[1,1326]{1,0:T(1,128)} %get-tuple-element.99.live_ref), custom_call_target="tpu_custom_call" | custom-call | flops 507510784 | bytes 7929856 | tf_op jit(solution)/shard_map/cond/branch_0_fun/payoff/pallas_call | solution.py:59
  13.3 0.8 %collective-permute-done.odd_ref = f32[11,24,128]{2,1,0:T(8,128)S(1)} collective-permute-done((f32[11,24,128]{2,1,0:T(8,128)S(1)}, f32[11,24,128]{2,1,0:T(8,128)S(1)}, u32[]{:S(2)}, u32[]{:S(2)}) %collective-permute-start) | collective-permute-done | bytes 135200 | tf_op jit(solution)/shard_map/cond/branch_0_fun/ppermute | solution.py:272
  14.2 1.4 %collective-permute-done.1.even_ref = f32[11,24,128]{2,1,0:T(8,128)S(1)} collective-permute-done((f32[11,24,128]{2,1,0:T(8,128)S(1)}, f32[11,24,128]{2,1,0:T(8,128)S(1)}, u32[]{:S(2)}, u32[]{:S(2)}) %collective-permute-start.1) | collective-permute-done | bytes 135200 | tf_op jit(solution)/shard_map/cond/branch_0_fun/ppermute | solution.py:272
  15.5 0.0 copy-done.4
  15.5 0.0 copy-done.8
  15.5 0.0 copy-start
  15.5 2.5 %first.4 = (f32[4,3,8,1408]{3,2,1,0:T(8,128)S(1)}, f32[4,4,8,1408]{3,2,1,0:T(8,128)S(1)}, f32[1,128]{1,0:T(1,128)S(1)}) custom-call(s32[8,128]{1,0:T(8,128)S(1)} %get-tuple-element.88.shift_ref, f32[4,11,3,8,128]{4,3,2,1,0:T(8,128)S(1)} %get-tuple-element.89.home_ref, f32[11,24,128]{2,1,0:T(8,128)S(1)} %collective-permute-done.odd_ref, ...), custom_call_target="tpu_custom_call" | custom-call | flops 1395654656 | bytes 11894784 | tf_op jit(solution)/shard_map/cond/branch_0_fun/first/pallas_call | solution.py:666
  18.1 11.3 %all_to_all.48 = f32[32,1,128]{2,1,0:T(1,128)S(1)} all-to-all(f32[32,1,128]{2,1,0:T(1,128)S(1)} %broadcast_in_dim.12), channel_id=1, replica_groups=mesh['node'=16,'board'=2] {'node','board'}, dimensions={0} | all-to-all | bytes 32768 | tf_op jit(solution)/shard_map/cond/branch_0_fun/all_to_all | solution.py:607
  29.4 2.3 %second.4 = (f32[4,11,4,8,128]{4,3,2,1,0:T(8,128)S(1)}, f32[11,32,128]{2,1,0:T(8,128)S(1)}, f32[11,32,128]{2,1,0:T(8,128)S(1)}, f32[1,128]{1,0:T(1,128)S(1)}) custom-call(s32[8,128]{1,0:T(8,128)S(1)} %get-tuple-element.88.shift_ref, f32[4,3,8,1408]{3,2,1,0:T(8,128)S(1)} %get-tuple-element.100.chain_ref, f32[4,4,8,1408]{3,2,1,0:T(8,128)S(1)} %get-tuple-element.101.value_ref, ...), custom_call_target="tpu_custom_call" | custom-call | flops 1141899264 | bytes 11894784 | tf_op jit(solution)/shard_map/cond/branch_0_fun/second/pallas_call | solution.py:680
  31.7 0.6 %collective-permute-start.2 = (f32[11,32,128]{2,1,0:T(8,128)S(1)}, f32[11,32,128]{2,1,0:T(8,128)S(1)}, u32[]{:S(2)}, u32[]{:S(2)}) collective-permute-start(f32[11,32,128]{2,1,0:T(8,128)S(1)} %get-tuple-element.104), channel_id=1, source_target_pairs={{0,2},{2,0},{4,6},{6,4},{8,10},{10,8},{12,14},{14,12},{16,18},{18,... | collective-permute-start | bytes 540680 | tf_op jit(solution)/shard_map/cond/branch_0_fun/ppermute | solution.py:272
  32.3 1.5 %collective-permute-start.3 = (f32[11,32,128]{2,1,0:T(8,128)S(1)}, f32[11,32,128]{2,1,0:T(8,128)S(1)}, u32[]{:S(2)}, u32[]{:S(2)}) collective-permute-start(f32[11,32,128]{2,1,0:T(8,128)S(1)} %get-tuple-element.105), channel_id=1, source_target_pairs={{2,4},{4,2},{6,8},{8,6},{10,12},{12,10},{14,16},{16,14},{18,20},{2... | collective-permute-start | bytes 540680 | tf_op jit(solution)/shard_map/cond/branch_0_fun/ppermute | solution.py:272
  33.8 11.5 %all_to_all.49 = f32[32,1,128]{2,1,0:T(1,128)S(1)} all-to-all(f32[32,1,128]{2,1,0:T(1,128)S(1)} %broadcast_in_dim.13), channel_id=1, replica_groups=mesh['node'=16,'board'=2] {'node','board'}, dimensions={0} | all-to-all | bytes 32768 | tf_op jit(solution)/shard_map/cond/branch_0_fun/all_to_all | solution.py:607
  45.3 0.0 collective-permute-done.2.even_ref
  45.3 0.0 collective-permute-done.3.odd_ref
  45.3 0.0 copy-done
  45.3 2.4 %last.4 = (f32[1,4,32,1326]{3,2,1,0:T(8,128)}, f32[1,4,32,1326]{3,2,1,0:T(8,128)}) custom-call(s32[8,128]{1,0:T(8,128)S(1)} %get-tuple-element.88.shift_ref, f32[4,11,4,8,128]{4,3,2,1,0:T(8,128)S(1)} %get-tuple-element.103.own_ref, f32[11,32,128]{2,1,0:T(8,128)S(1)} %collective-permute-done.2.even_ref, f32[11,32,128]{2,1,0:T(8,128)S(1)} %collective-permute-done.3.odd_ref, ...), custom_call_target="tpu_custom_call" | custom-call | tf_op jit(solution)/shard_map/cond/branch_0_fun/last/pallas_call | solution.py:695
  (2 shorter events, 0.0 us)
Async XLA Ops:
  3.1 12.4 %copy-start.4 = (f32[1,1326]{1,0:T(1,128)S(1)}, f32[1,1326]{1,0:T(1,128)}, u32[]{:S(2)}) copy-start(f32[1,1326]{1,0:T(1,128)} %get-tuple-element.95.rest_0_.rest_1_) | copy-start | bytes 15916 | tf_op jit(solution)/shard_map/cond
  3.1 12.4 %copy-start.8 = (f32[1,1326]{1,0:T(1,128)S(1)}, f32[1,1326]{1,0:T(1,128)}, u32[]{:S(2)}) copy-start(f32[1,1326]{1,0:T(1,128)} %get-tuple-element.96.rest_1_.rest_2_) | copy-start | bytes 15916 | tf_op jit(solution)/shard_map/cond
  3.5 10.7 %collective-permute-start = (f32[11,24,128]{2,1,0:T(8,128)S(1)}, f32[11,24,128]{2,1,0:T(8,128)S(1)}, u32[]{:S(2)}, u32[]{:S(2)}) collective-permute-start(f32[11,24,128]{2,1,0:T(8,128)S(1)} %get-tuple-element.93), channel_id=1, source_target_pairs={{2,4},{4,2},{6,8},{8,6},{10,12},{12,10},{14,16},{16,14},{18,20},{2... | collective-permute-start | bytes 405512 | tf_op jit(solution)/shard_map/cond/branch_0_fun/ppermute | solution.py:272
  10.5 5.0 %collective-permute-start.1 = (f32[11,24,128]{2,1,0:T(8,128)S(1)}, f32[11,24,128]{2,1,0:T(8,128)S(1)}, u32[]{:S(2)}, u32[]{:S(2)}) collective-permute-start(f32[11,24,128]{2,1,0:T(8,128)S(1)} %get-tuple-element.94), channel_id=1, source_target_pairs={{0,2},{2,0},{4,6},{6,4},{8,10},{10,8},{12,14},{14,12},{16,18},{18,... | collective-permute-start | bytes 405512 | tf_op jit(solution)/shard_map/cond/branch_0_fun/ppermute | solution.py:272
  15.5 29.8 %copy-start = (f32[1,4,32,1326]{3,2,1,0:T(8,128)S(1)}, f32[1,4,32,1326]{3,2,1,0:T(8,128)}, u32[]{:S(2)}) copy-start(f32[1,4,32,1326]{3,2,1,0:T(8,128)} %get-tuple-element.107.rest_1_) | copy-start | bytes 2036740 | tf_op jit(solution)/shard_map/cond
  31.7 13.6 %collective-permute-start.2 = (f32[11,32,128]{2,1,0:T(8,128)S(1)}, f32[11,32,128]{2,1,0:T(8,128)S(1)}, u32[]{:S(2)}, u32[]{:S(2)}) collective-permute-start(f32[11,32,128]{2,1,0:T(8,128)S(1)} %get-tuple-element.104), channel_id=1, source_target_pairs={{0,2},{2,0},{4,6},{6,4},{8,10},{10,8},{12,14},{14,12},{16,18},{18,... | collective-permute-start | bytes 540680 | tf_op jit(solution)/shard_map/cond/branch_0_fun/ppermute | solution.py:272
  32.3 13.0 %collective-permute-start.3 = (f32[11,32,128]{2,1,0:T(8,128)S(1)}, f32[11,32,128]{2,1,0:T(8,128)S(1)}, u32[]{:S(2)}, u32[]{:S(2)}) collective-permute-start(f32[11,32,128]{2,1,0:T(8,128)S(1)} %get-tuple-element.105), channel_id=1, source_target_pairs={{2,4},{4,2},{6,8},{8,6},{10,12},{12,10},{14,16},{16,14},{18,20},{2... | collective-permute-start | bytes 540680 | tf_op jit(solution)/shard_map/cond/branch_0_fun/ppermute | solution.py:272
